TPU v7x, 512 devices: a whole 4x4x16 slice. The times are simulated.
512 devices in a mesh: tm: 16 (over x, y), rows: 32 (over z, core).
Axes of the slice: x: 4, y: 4, z: 16, core: 2. Of those that a mesh axis runs over, the one named last changes fastest.
Arguments:
- queries: bfloat16 [16, 64, 128, 1152], P('tm', 'rows'), may hold values from -6 to 6
- keys: bfloat16 [16, 64, 128, 1152], P('tm', 'rows'), may hold values from -18 to 18
- values: bfloat16 [16, 64, 128, 1152], P('tm', 'rows'), may hold values from -4.8 to 12
- cotangent: bfloat16 [16, 64, 128, 1152], P('tm', 'rows'), may hold values from -6 to 6
- kernel: float32 [3, 3, 1152], replicated, may hold values from -1.2 to 1.2
Outputs:
- grad_queries: bfloat16 [16, 64, 128, 1152], P('tm', 'rows')
- grad_keys: bfloat16 [16, 64, 128, 1152], P('tm', 'rows')
- grad_values: bfloat16 [16, 64, 128, 1152], P('tm', 'rows')
- grad_kernel: float32 [3, 3, 1152], replicated
All inputs are finite; a program needn't handle non-finite values.
Results may differ from a plain program's by a relative error of at most 0.008.
Values may be sent and summed in bfloat16 or wider, within the bound.
A program may use at most 64 MiB of HBM per device.

v0:
```python
import jax
import jax.numpy as jnp
from jax import lax
from jax.sharding import PartitionSpec as P

HEADS = 36
HEAD_DIM = 32


DEN_EPS = 0.1
HIGH = lax.Precision.HIGHEST


def padded_2(value, sides, width):
    for axis, dim in sides:
        size, length = (lax.axis_size(axis), value.shape[dim])
        up = [(i, (i + 1) % size) for i in range(size - 1)]
        down = [(j, i) for i, j in up]
        last = lax.slice_in_dim(value, length - width, length, axis=dim)
        leading = lax.slice_in_dim(value, 0, width, axis=dim)
        before = lax.ppermute(last, axis, up)
        after = lax.ppermute(leading, axis, down)
        value = jnp.concatenate([before, value, after], axis=dim)
    return value


def conv_terms(values, cotangent, kernel, grad_pad, value_pad):
    rows_here = values.shape[1]
    cols_here = values.shape[2]
    grad_wide = cotangent.astype(jnp.float32)
    dv_conv = jnp.zeros(values.shape, jnp.float32)
    kernel_rows = []
    for a in (-1, 0, 1):
        kernel_cols = []
        for b in (-1, 0, 1):
            shifted = grad_pad[:, 1 - a : 1 - a + rows_here, 1 - b : 1 - b + cols_here, :]
            dv_conv = dv_conv + kernel[a + 1, b + 1] * shifted
            moved = value_pad[:, 1 + a : 1 + a + rows_here, 1 + b : 1 + b + cols_here, :]
            product = moved * grad_wide
            kernel_cols.append(jnp.sum(product, axis=(0, 1, 2)))
        kernel_rows.append(jnp.stack(kernel_cols))
    return (dv_conv, jnp.stack(kernel_rows))


def pad_columns(x, dim):
    widths = [(0, 0)] * x.ndim
    widths[dim] = (1, 1)
    return jnp.pad(x, widths)


def shards(queries, keys, values, cotangent, kernel):
    shape = queries.shape
    tokens_here = shape[0] * shape[1] * shape[2]
    total = tokens_here * lax.axis_size("tm") * lax.axis_size("rows")
    q_flat = queries.reshape(tokens_here, HEADS, HEAD_DIM)
    k_flat = keys.reshape(tokens_here, HEADS, HEAD_DIM)
    v_flat = values.reshape(tokens_here, HEADS, HEAD_DIM)
    g_flat = cotangent.reshape(tokens_here, HEADS, HEAD_DIM).astype(jnp.float32)
    pos_q = jnp.maximum(q_flat, 0)
    pos_k = jnp.maximum(k_flat, 0)
    part_states = jnp.einsum("nhe,nhf->hef", pos_k, v_flat, preferred_element_type=jnp.float32)
    part_keysum = jnp.sum(pos_k, axis=0, dtype=jnp.float32)
    states, keysum = lax.psum((part_states, part_keysum), ("tm", "rows"))
    states = states / total
    keysum = keysum / total
    stacked = jnp.stack((cotangent, values))
    padded = padded_2(stacked, (("rows", 2),), 1)
    padded = pad_columns(padded, 3).astype(jnp.float32)
    dv_conv, kernel_term = conv_terms(values, cotangent, kernel, padded[0], padded[1])
    grad_kernel = lax.psum(kernel_term, ("tm", "rows"))
    pos_qf = pos_q.astype(jnp.float32)
    den = jnp.einsum("nhe,he->nh", pos_qf, keysum, precision=HIGH) + DEN_EPS
    num = jnp.einsum("nhe,hef->nhf", pos_qf, states, precision=HIGH)
    dnum = g_flat / den[:, :, None]
    dden = -jnp.sum(g_flat * num, axis=2) / (den * den)
    dpos_q = (
        jnp.einsum("nhf,hef->nhe", dnum, states, precision=HIGH) + dden[:, :, None] * keysum[None]
    )
    grad_queries = jnp.where(q_flat > 0, dpos_q, 0.0).astype(jnp.bfloat16).reshape(shape)
    part_gstate = jnp.einsum("nhe,nhf->hef", pos_qf, dnum, precision=HIGH)
    part_gkeysum = jnp.einsum("nhe,nh->he", pos_qf, dden, precision=HIGH)
    gstate, gkeysum = lax.psum((part_gstate, part_gkeysum), ("tm", "rows"))
    v_wide = v_flat.astype(jnp.float32)
    dpos_k = (jnp.einsum("hef,nhf->nhe", gstate, v_wide, precision=HIGH) + gkeysum[None]) / total
    grad_keys = jnp.where(k_flat > 0, dpos_k, 0.0).astype(jnp.bfloat16).reshape(shape)
    dv_attn = jnp.einsum("nhe,hef->nhf", pos_k.astype(jnp.float32), gstate, precision=HIGH) / total
    grad_values = (dv_attn.reshape(shape) + dv_conv).astype(jnp.bfloat16)
    return (grad_queries, grad_keys, grad_values, grad_kernel)


def solution(mesh):
    placed = (
        P("tm", "rows", None, None),
        P("tm", "rows", None, None),
        P("tm", "rows", None, None),
        P("tm", "rows", None, None),
        P(),
    )
    return jax.shard_map(
        shards,
        mesh=mesh,
        in_specs=placed,
        out_specs=(
            P("tm", "rows", None, None),
            P("tm", "rows", None, None),
            P("tm", "rows", None, None),
            P(),
        ),
        check_vma=False,
    )
```

profile of v0, /device:TPU:1, one launch (start us, length us, event | category | flops | bytes accessed | tf_op | source)
XLA Modules:
  0.0 751.5 jit_solution(9182392818282554306)
XLA Ops:
  7.2 0.0 all-reduce.5.cloned.1.call-start
  7.2 0.0 copy-start
  7.2 2.4 fusion.34
  9.7 5.1 collective-permute-start
  14.7 5.9 collective-permute-start.1
  20.7 0.0 copy-done
  20.7 0.6 copy.26
  21.3 0.0 copy-start.1
  21.3 0.1 convert_reduce_fusion
  21.5 0.0 copy-start.5
  21.5 0.9 broadcast_maximum_fusion.1
  22.3 0.0 copy-done.1
  22.4 1.7 copy.25
  24.1 0.9 broadcast_maximum_fusion
  25.0 2.9 copy.27
  27.9 2.1 max.16
  30.0 0.7 reduce_sum.102
  30.7 105.8 %psum.36 = f32[36,32]{1,0:T(8,128)} all-reduce(f32[36,32]{1,0:T(8,128)} %reduce_sum.102), channel_id=1, replica_groups=mesh['tm'=16,'rows'=32] {'tm','rows'}, use_global_device_ids=true, to_apply=%region_2.0 | all-reduce | flops 1152 | bytes 9216 | tf_op jit(solution)/shard_map/psum | solution.py:63
  136.6 1.3 fusion.47
  137.9 0.4 fusion.43
  138.3 0.6 copy-done.10
  138.9 0.6 fusion.40
  139.5 2.0 reshape.69
  141.5 2.2 copy.24
  143.7 0.4 max.14
  144.1 2.1 reshape.65
  146.2 3.1 fusion.37
  149.3 1.1 fusion.48
  150.4 0.0 all-reduce.5.cloned.1.call-update
  150.4 0.9 broadcast_compare_fusion
  151.3 0.2 copy-done.6
  151.5 0.9 broadcast_compare_fusion.1
  152.3 2.5 copy.29
  154.9 0.0 copy-start.21
  154.9 1.6 gt.15
  156.5 1.1 copy.23
  157.6 1.6 gt.13
  159.2 0.0 copy-done.21
  159.2 0.7 slice_reduce_fusion.8
  159.9 454.3 %all-reduce.5.cloned.1.call-done = (f32[36,32,32]{2,1,0:T(8,128)}, f32[36,32,32]{2,1,0:T(8,128)}) async-done(((f32[36,32,32]{2,1,0:T(8,128)}, f32[36,32,32]{2,1,0:T(8,128)}), (f32[36,32,32]{2,1,0:T(8,128)}, f32[36,32,32]{2,1,0:T(8,128)})) %all-reduce.5.cloned.1.call-update) | async-done | bytes 294928 | tf_op jit(solution)/shard_map/psum | solution.py:63
  614.2 2.3 fusion.14
  616.5 0.0 copy-done.11
  616.5 0.0 copy-start.13
  616.5 0.6 fusion.41
  617.1 0.6 copy.48
  617.7 0.7 fusion.8
  618.4 0.6 reshape.68
  619.0 2.0 copy.31
  621.0 2.5 fusion.13
  623.5 0.1 reshape.66
  623.6 1.7 copy.32
  625.4 0.0 collective-permute-done
  625.4 0.0 collective-permute-done.1
  625.4 2.5 fusion.1
  627.8 0.3 slice_bitcast_fusion.1
  628.2 0.0 copy-start.12
  628.2 1.1 fusion.15
  629.5 105.6 %all-reduce.1 = (f32[36,32]{1,0:T(8,128)S(1)}, f32[3,3,1152]{2,1,0:T(4,128)}) all-reduce(f32[36,32]{1,0:T(8,128)S(1)} %bitcast.82, f32[3,3,1152]{2,1,0:T(4,128)S(1)} %pad_maximum_fusion.1), channel_id=1, replica_groups=mesh['tm'=16,'rows'=32] {'tm','rows'}, use_global_device_ids=true, to_apply=%region_5.6 | all-reduce | flops 11520 | bytes 92160 | tf_op jit(solution)/shard_map/psum | solution.py:82
  735.1 2.8 fusion.12
  737.9 0.0 copy-start.18
  737.9 0.0 copy-start.19
  737.9 1.9 reshape.67
  739.8 1.7 copy.33
  741.6 3.1 fusion.26
  (43 shorter events, 0.2 us)
Async XLA Ops:
  7.2 607.0 %all-reduce.5.cloned.1.call-start = ((), (), s32[]{:S(2)}) async-start(), calls=%async_computation | async-start | bytes 2359296 | tf_op jit(solution)/shard_map/psum | solution.py:63
  7.2 13.5 %copy-start = (bf16[1,2,128,1152]{3,2,1,0:T(8,128)(2,1)S(1)}, bf16[1,2,128,1152]{3,2,1,0:T(8,128)(2,1)}, u32[]{:S(2)}) copy-start(bf16[1,2,128,1152]{3,2,1,0:T(8,128)(2,1)} %param.8) | copy-start | bytes 1769476
  9.7 11.7 %copy-start.2 = (bf16[1,2,128,1152]{3,2,1,0:T(8,128)(2,1)S(1)}, bf16[1,2,128,1152]{3,2,1,0:T(8,128)(2,1)}, u32[]{:S(2)}) copy-start(bf16[1,2,128,1152]{3,2,1,0:T(8,128)(2,1)} %param.6) | copy-start | bytes 1769476
  9.7 615.7 %collective-permute-start = (bf16[2,1,1,128,1152]{4,3,2,1,0:T(8,128)(2,1)}, bf16[2,1,1,128,1152]{4,3,2,1,0:T(8,128)(2,1)}, u32[]{:S(2)}, u32[]{:S(2)}) collective-permute-start(bf16[2,1,1,128,1152]{4,3,2,1,0:T(8,128)(2,1)} %get-tuple-element.36), channel_id=1, source_target_pairs={{0,1},{1,2},{2,3},{3,4},{4,5},{5,6},{6,7},{7,8},{8,9},{9,10},{10,1... | collective-permute-start | bytes 1769480 | tf_op jit(solution)/shard_map/ppermute | solution.py:21
  14.7 610.6 %collective-permute-start.1 = (bf16[2,1,1,128,1152]{4,3,2,1,0:T(8,128)(2,1)}, bf16[2,1,1,128,1152]{4,3,2,1,0:T(8,128)(2,1)}, u32[]{:S(2)}, u32[]{:S(2)}) collective-permute-start(bf16[2,1,1,128,1152]{4,3,2,1,0:T(8,128)(2,1)} %get-tuple-element.37), channel_id=1, source_target_pairs={{1,0},{2,1},{3,2},{4,3},{5,4},{6,5},{7,6},{8,7},{9,8},{10,9},{11,1... | collective-permute-start | bytes 1769480 | tf_op jit(solution)/shard_map/ppermute | solution.py:22
  21.3 1.1 copy-start.1
  21.5 2.7 copy-start.5
  138.3 0.6 copy-start.10
  146.2 3.1 copy-start.3
  150.4 1.1 copy-start.6
  152.3 4.1 copy-start.8
  154.9 4.3 copy-start.21
  614.2 2.3 copy-start.11
  614.2 3.5 copy-start.7
  616.5 1.2 copy-start.13
  619.0 2.0 copy-start.4
  628.2 1.3 copy-start.12
  628.2 106.9 %copy-start.9 = (pred[256,36,32]{0,2,1:T(32,128)(4,1)S(1)}, pred[256,36,32]{0,2,1:T(32,128)(4,1)}, u32[]{:S(2)}) copy-start(pred[256,36,32]{0,2,1:T(32,128)(4,1)} %gt.15) | copy-start | bytes 884740
  737.9 3.6 copy-start.14
  737.9 3.6 copy-start.15
  737.9 3.6 copy-start.16
  737.9 3.6 copy-start.17
  737.9 3.6 copy-start.18
  737.9 3.6 copy-start.19
  737.9 3.6 copy-start.20
Sparse Core Ops, SparseCore 0:
  150.5 463.6 all-reduce.4
where the time goes:
time: 752 us
  waiting for transfers between devices  454 us (60%)
  blocking collectives  211 us (28%)
  local copies, waits for them, and re-layouts  32.1 us (4%)
  other arithmetic  14.8 us (2%)
  between operations  14.5 us (2%)
  matrix products  13.3 us (2%)
  starting transfers between devices  11 us (1%)
    psum x1, waiting for transfers between devices, shards(): states, keysum = lax.psum((part_states, part_keysum), ('tm', 'rows'))  454 us
    psum x1, blocking collectives, shards(): states, keysum = lax.psum((part_states, part_keysum), ('tm', 'rows'))  106 us
    psum x1, blocking collectives, shards(): gstate, gkeysum = lax.psum((part_gstate, part_gkeysum), ('tm', 'rows'))  106 us
  transfers between devices with their start and end apart: 3, of which 1 were waited for; matrix products, arithmetic and copies ran while one was open for 6% of the time, Pallas kernels for 0%

commit v1 on v0

v1 whole, which is shorter than its diff:
```python
import functools

import jax
import jax.numpy as jnp
from jax import lax
from jax.experimental import pallas as pl
from jax.experimental.pallas import tpu as pltpu
from jax.sharding import PartitionSpec as P

MESH = pl.DeviceIdType.MESH
F32 = jnp.float32
BF16 = jnp.bfloat16

HEADS = 36
HEAD_DIM = 32
DEN_EPS = 0.1

LANES = 128
CHANNELS = HEADS * HEAD_DIM
GROUPS = CHANNELS // LANES
PACK = 16
STATE_CHUNKS = GROUPS * HEAD_DIM // PACK
ALL_CHUNKS = STATE_CHUNKS + GROUPS


def lanes(group):
    return pl.ds(group * LANES, LANES)


def block_mask():
    row = lax.broadcasted_iota(jnp.int32, (LANES, LANES), 0)
    col = lax.broadcasted_iota(jnp.int32, (LANES, LANES), 1)
    return (row // HEAD_DIM) == (col // HEAD_DIM)


def pack_heads(full):
    col = lax.broadcasted_iota(jnp.int32, (HEAD_DIM, LANES), 1) // HEAD_DIM
    out = full[0:HEAD_DIM]
    for h in range(1, LANES // HEAD_DIM):
        out = jnp.where(col == h, full[h * HEAD_DIM : (h + 1) * HEAD_DIM], out)
    return out


def unpack_heads(packed, mask):
    tiled = jnp.concatenate([packed.astype(F32)] * (LANES // HEAD_DIM), axis=0)
    return jnp.where(mask, tiled, 0.0)


def split(x):
    high = x.astype(BF16)
    return jnp.concatenate([high, (x - high.astype(F32)).astype(BF16)], axis=1)


def total(slots):
    return jnp.sum(slots.astype(F32), axis=0)


def exchange_kernel(
    sizes,
    q_hbm,
    k_hbm,
    v_hbm,
    g_hbm,
    w_hbm,
    gq_hbm,
    conv_hbm,
    sums_out,
    gks_out,
    kb,
    vb,
    qb,
    gb,
    w_ref,
    halo,
    inv_den,
    conv,
    gq,
    ks_plane,
    ks_line,
    st_src,
    st_rs,
    st_line,
    st_all,
    gs_src,
    gs_rs,
    gs_line,
    gs_all,
    gk_plane,
    gk_line,
    load_sem,
    store_sem,
    halo_send,
    halo_recv,
    send_sem,
    recv_sem,
    relay_sem,
):
    tm_size, rows_size = sizes
    plane_size, line_size = tm_size * 2, rows_size // 2
    count = kb.shape[0] * tm_size * rows_size
    width = kb.shape[0] // 2
    tm = lax.axis_index("tm")
    r = lax.axis_index("rows")
    z, core = r // 2, r % 2
    me = core * tm_size + tm

    def in_plane(i):
        return (i % tm_size, z * 2 + i // tm_size)

    def in_line(i):
        return (tm, i * 2 + core)

    loads = [
        pltpu.make_async_copy(src, dst, load_sem.at[i])
        for i, (src, dst) in enumerate(
            ((k_hbm, kb), (v_hbm, vb), (q_hbm, qb), (g_hbm, gb), (w_hbm, w_ref))
        )
    ]
    for load in loads:
        load.start()

    barrier = pltpu.get_barrier_semaphore()

    def greet(device):
        pl.semaphore_signal(barrier, inc=1, device_id=device, device_id_type=MESH)

    def greet_plane(d, _):
        greet(in_plane((me + d) % plane_size))
        return 0

    def greet_line(d, _):
        greet(in_line((z + 1 + d + (d // 4) * (line_size - 9)) % line_size))
        return 0

    lax.fori_loop(1, plane_size, greet_plane, 0)
    lax.fori_loop(0, 8, greet_line, 0)
    greet((tm, (r + 2 * core + rows_size - 1) % rows_size))

    def remote(src, dst, which, device):
        return pltpu.make_async_remote_copy(
            src_ref=src,
            dst_ref=dst,
            send_sem=send_sem.at[which],
            recv_sem=recv_sem.at[which],
            device_id=device,
            device_id_type=MESH,
        )

    def to_plane(buf, slot, which):
        def send(d, _):
            remote(buf.at[slot], buf.at[slot], which, in_plane((me + d) % plane_size)).start()
            return 0

        lax.fori_loop(1, plane_size, send, 0)

    def to_line(buf, which):
        def send(d, _):
            far = (z + line_size // 2 + (1 - 2 * (d % 2)) * ((d + 1) // 2) + line_size) % line_size
            remote(buf.at[z], buf.at[z], which, in_line(far)).start()
            return 0

        lax.fori_loop(0, line_size - 1, send, 0)

    def to_owners(src, dst, chunks, which):
        def send(i, _):
            owner = (me + i) % chunks

            @pl.when(owner != me)
            def _():
                remote(src.at[owner], dst.at[me], which, in_plane(owner)).start()

            return 0

        lax.fori_loop(0, chunks, send, 0)

        @pl.when(me < chunks)
        def _():
            dst[me] = src[me]

    def arrived(buf, n, sem):
        view = buf.at[pl.ds(0, n)]
        pltpu.make_async_copy(view, view, sem).wait()

    def all_arrived(buf, chunks, which):
        @pl.when(me < chunks)
        def _():
            arrived(buf, chunks - 1, recv_sem.at[which])

        @pl.when(me >= chunks)
        def _():
            arrived(buf, chunks, recv_sem.at[which])

    KS1, KS2, ST1, ST2, ST3, GS1, GS2, GS3, GK1, GK2 = range(10)
    mask = block_mask()
    ones_block = jnp.where(mask, 1.0, 0.0).astype(BF16)
    ones_twice = jnp.concatenate([ones_block, ones_block], axis=0)
    row16 = lax.broadcasted_iota(jnp.int32, (PACK, LANES), 0)

    loads[0].wait()
    ks_rows = jnp.zeros((PACK, LANES), F32)
    for i in range(GROUPS):
        pk = jnp.maximum(kb[:, i * LANES : (i + 1) * LANES], 0)
        ones = jnp.ones((PACK, kb.shape[0]), BF16)
        ks = jnp.dot(ones, pk, preferred_element_type=F32)
        ks_rows = jnp.where(row16 == i, ks, ks_rows)
    ks_plane[me] = ks_rows.astype(BF16)
    loads[1].wait()
    for i in range(GROUPS):
        pk = jnp.maximum(kb[:, i * LANES : (i + 1) * LANES], 0)
        full = lax.dot_general(
            pk,
            vb[:, i * LANES : (i + 1) * LANES],
            (((0,), (0,)), ((), ())),
            preferred_element_type=F32,
        )
        st_src[2 * i : 2 * i + 2] = pack_heads(full).astype(BF16).reshape(2, PACK, LANES)

    pl.semaphore_wait(barrier, plane_size + 8)
    to_plane(ks_plane, me, KS1)
    to_owners(st_src, st_rs, STATE_CHUNKS, ST1)
    for d in (4, line_size - 4):
        pl.semaphore_signal(
            relay_sem, inc=1, device_id=in_line((z + d) % line_size), device_id_type=MESH
        )

    loads[3].wait()

    def to_before():
        return pltpu.make_async_remote_copy(
            src_ref=gb.at[pl.ds(0, width)],
            dst_ref=halo.at[1],
            send_sem=halo_send.at[0],
            recv_sem=halo_recv.at[1],
            device_id=(tm, r - 1),
            device_id_type=MESH,
        )

    def to_after():
        return pltpu.make_async_remote_copy(
            src_ref=gb.at[pl.ds(width, width)],
            dst_ref=halo.at[0],
            send_sem=halo_send.at[1],
            recv_sem=halo_recv.at[0],
            device_id=(tm, r + 1),
            device_id_type=MESH,
        )

    @pl.when(r > 0)
    def _():
        to_before().start()

    @pl.when(r == 0)
    def _():
        halo[0] = jnp.zeros(halo.shape[1:], BF16)

    @pl.when(r < rows_size - 1)
    def _():
        to_after().start()

    @pl.when(r == rows_size - 1)
    def _():
        halo[1] = jnp.zeros(halo.shape[1:], BF16)

    arrived(ks_plane, plane_size - 1, recv_sem.at[KS1])
    ks_line[z] = total(ks_plane[...]).astype(BF16)
    pl.semaphore_wait(relay_sem, 2)
    to_line(ks_line, KS2)

    @pl.when(me < STATE_CHUNKS)
    def _():
        arrived(st_rs, plane_size - 1, recv_sem.at[ST1])
        st_line[z] = total(st_rs[...]).astype(BF16)
        to_line(st_line, ST2)

    @pl.when(r > 0)
    def _():
        pltpu.make_async_copy(halo.at[0], halo.at[0], halo_recv.at[0]).wait()

    @pl.when(r < rows_size - 1)
    def _():
        pltpu.make_async_copy(halo.at[1], halo.at[1], halo_recv.at[1]).wait()

    loads[4].wait()

    def conv_group(i, _):
        at = pl.ds(pl.multiple_of(i * LANES, LANES), LANES)
        col = lax.broadcasted_iota(jnp.int32, (width, LANES), 0)
        grads = (halo[0, :, at], gb[0:width, at], gb[width:, at], halo[1, :, at])
        vals = [vb[0:width, at].astype(F32), vb[width:, at].astype(F32)]
        out = [jnp.zeros((width, LANES), F32) for _ in range(2)]
        taps = [jnp.zeros((8, LANES), F32) for _ in range(9)]
        for s in range(4):
            base = grads[s].astype(F32)
            for b in (-1, 0, 1):
                if b == 1:
                    moved = jnp.where(col == 0, 0.0, pltpu.roll(base, 1, 0))
                elif b == -1:
                    moved = jnp.where(col == width - 1, 0.0, pltpu.roll(base, width - 1, 0))
                else:
                    moved = base
                for j in range(2):
                    a = j + 1 - s
                    if -1 <= a <= 1:
                        tap = (a + 1) * 3 + b + 1
                        out[j] = out[j] + w_ref[a + 1, b + 1 : b + 2, at] * moved
                        product = (vals[j] * moved).reshape(width // 8, 8, LANES)
                        taps[tap] = taps[tap] + jnp.sum(product, axis=0)
        conv[0:width, at] = out[0]
        conv[width:, at] = out[1]
        rows = jnp.zeros((PACK, LANES), F32)
        for tap in range(9):
            rows = jnp.where(row16 == tap, jnp.sum(taps[tap], axis=0, keepdims=True), rows)
        gs_src[STATE_CHUNKS + i] = rows.astype(BF16)
        return 0

    lax.fori_loop(0, GROUPS, conv_group, 0)
    conv_store = pltpu.make_async_copy(conv, conv_hbm, store_sem.at[0])
    conv_store.start()

    loads[2].wait()
    arrived(ks_line, line_size - 1, recv_sem.at[KS2])
    keysum = total(ks_line[...]) * (1.0 / count)
    for i in range(GROUPS):
        at = slice(i * LANES, (i + 1) * LANES)
        pq = jnp.maximum(qb[:, at], 0)
        weighted = split(pq.astype(F32) * keysum[i : i + 1])
        den = jnp.dot(weighted, ones_twice, preferred_element_type=F32) + DEN_EPS
        inv = 1.0 / den
        inv_den[:, at] = inv
        dnum = (gb[:, at].astype(F32) * inv).astype(BF16)
        full = lax.dot_general(
            pq, dnum, (((0,), (0,)), ((), ())), preferred_element_type=F32
        )
        gs_src[2 * i : 2 * i + 2] = pack_heads(full).astype(BF16).reshape(2, PACK, LANES)
    to_owners(gs_src, gs_rs, ALL_CHUNKS, GS1)

    @pl.when(me < STATE_CHUNKS)
    def _():
        arrived(st_line, line_size - 1, recv_sem.at[ST2])
        st_all[me] = total(st_line[...]) * (1.0 / count)
        to_plane(st_all, me, ST3)

    @pl.when(me < ALL_CHUNKS)
    def _():
        arrived(gs_rs, plane_size - 1, recv_sem.at[GS1])
        gs_line[z] = total(gs_rs[...]).astype(BF16)
        to_line(gs_line, GS2)

    all_arrived(st_all, STATE_CHUNKS, ST3)
    gks_rows = jnp.zeros((PACK, LANES), F32)
    for i in range(GROUPS):
        at = slice(i * LANES, (i + 1) * LANES)
        state = split(unpack_heads(st_all[2 * i : 2 * i + 2].reshape(HEAD_DIM, LANES), mask))
        grad = gb[:, at]
        pq = jnp.maximum(qb[:, at].astype(F32), 0.0)
        inv = inv_den[:, at]
        pulled = lax.dot_general(
            jnp.concatenate([grad, grad], axis=1),
            state,
            (((1,), (1,)), ((), ())),
            preferred_element_type=F32,
        )
        inner = jnp.dot(split(pq * pulled), ones_twice, preferred_element_type=F32)
        dden = -inner * (inv * inv)
        dq = pulled * inv + dden * keysum[i : i + 1]
        gq[:, at] = jnp.where(pq > 0, dq, 0.0).astype(BF16)
        part = jnp.sum(pq * dden, axis=0, keepdims=True)
        gks_rows = jnp.where(row16 == i, part, gks_rows)
    gk_plane[me] = gks_rows.astype(BF16)
    to_plane(gk_plane, me, GK1)
    gq_store = pltpu.make_async_copy(gq, gq_hbm, store_sem.at[1])
    gq_store.start()

    @pl.when(me < ALL_CHUNKS)
    def _():
        arrived(gs_line, line_size - 1, recv_sem.at[GS2])
        gs_all[me] = total(gs_line[...]).astype(BF16)
        to_plane(gs_all, me, GS3)

    arrived(gk_plane, plane_size - 1, recv_sem.at[GK1])
    gk_line[z] = total(gk_plane[...]).astype(BF16)
    to_line(gk_line, GK2)

    all_arrived(gs_all, ALL_CHUNKS, GS3)
    sums_out[...] = gs_all[...]
    arrived(gk_line, line_size - 1, recv_sem.at[GK2])
    gks_out[...] = total(gk_line[...])

    conv_store.wait()
    gq_store.wait()

    @pl.when(r > 0)
    def _():
        to_before().wait_send()

    @pl.when(r < rows_size - 1)
    def _():
        to_after().wait_send()

    for buf, which in ((ks_plane, KS1), (gk_plane, GK1)):
        arrived(buf, plane_size - 1, send_sem.at[which])
    for buf, which in ((ks_line, KS2), (gk_line, GK2)):
        arrived(buf, line_size - 1, send_sem.at[which])
    for chunks, src, rs, line, all_, first, second, third in (
        (STATE_CHUNKS, st_src, st_rs, st_line, st_all, ST1, ST2, ST3),
        (ALL_CHUNKS, gs_src, gs_rs, gs_line, gs_all, GS1, GS2, GS3),
    ):

        @pl.when(me < chunks)
        def _(chunks=chunks, src=src, rs=rs, line=line, all_=all_, first=first, second=second, third=third):
            arrived(src, chunks - 1, send_sem.at[first])
            arrived(line, line_size - 1, send_sem.at[second])
            for _ in range(all_.dtype.itemsize // rs.dtype.itemsize):
                arrived(rs, plane_size - 1, send_sem.at[third])

        @pl.when(me >= chunks)
        def _(chunks=chunks, src=src, first=first):
            arrived(src, chunks, send_sem.at[first])


def finish_kernel(
    count,
    k_hbm,
    v_hbm,
    conv_hbm,
    gq_hbm,
    sums,
    gks,
    gq_out,
    gk_out,
    gv_out,
    gw_out,
    kb,
    vb,
    conv,
    gk,
    gv,
    load_sem,
    store_sem,
):
    parts = 3
    wide = CHANNELS // parts
    pass_on = pltpu.make_async_copy(gq_hbm, gq_out, store_sem.at[0, parts])
    loads = []
    for p in range(parts):
        at = pl.ds(p * wide, wide)
        loads.append(
            [
                pltpu.make_async_copy(src.at[:, at], dst.at[:, at], load_sem.at[i, p])
                for i, (src, dst) in enumerate(((k_hbm, kb), (v_hbm, vb), (conv_hbm, conv)))
            ]
        )
    for part in loads:
        for load in part:
            load.start()
    pass_on.start()
    mask = block_mask()
    stores = []
    for p in range(parts):
        for load in loads[p]:
            load.wait()
        for i in range(p * (GROUPS // parts), (p + 1) * (GROUPS // parts)):
            at = slice(i * LANES, (i + 1) * LANES)
            grad = unpack_heads(sums[2 * i : 2 * i + 2].reshape(HEAD_DIM, LANES), mask).astype(BF16)
            keys = kb[:, at].astype(F32)
            dk = lax.dot_general(
                vb[:, at], grad, (((1,), (1,)), ((), ())), preferred_element_type=F32
            )
            dk = (dk + gks[i : i + 1]) * (1.0 / count)
            gk[:, at] = jnp.where(keys > 0, dk, 0.0).astype(BF16)
            dv = jnp.dot(jnp.maximum(kb[:, at], 0), grad, preferred_element_type=F32)
            gv[:, at] = (dv * (1.0 / count) + conv[:, at]).astype(BF16)
        at = pl.ds(p * wide, wide)
        for i, (src, dst) in enumerate(((gk, gk_out), (gv, gv_out))):
            store = pltpu.make_async_copy(src.at[:, at], dst.at[:, at], store_sem.at[i, p])
            store.start()
            stores.append(store)
    for i in range(GROUPS):
        at = slice(i * LANES, (i + 1) * LANES)
        rows = sums[STATE_CHUNKS + i].astype(F32)
        for a in range(3):
            gw_out[a, :, at] = rows[3 * a : 3 * a + 3]
    for store in stores:
        store.wait()
    pass_on.wait()


def shards(sizes, queries, keys, values, cotangent, kernel):
    shape = queries.shape
    tokens = shape[0] * shape[1] * shape[2]
    count = tokens * sizes[0] * sizes[1]
    flat = (tokens, CHANNELS)
    plane, line = sizes[0] * 2, sizes[1] // 2
    q, k, v, g = (x.reshape(flat) for x in (queries, keys, values, cotangent))
    q, k, v, g, w = (
        pltpu.with_memory_space_constraint(x, pltpu.HBM) for x in (q, k, v, g, kernel)
    )
    hbm = pl.BlockSpec(memory_space=pltpu.HBM)
    vmem = pl.BlockSpec(memory_space=pltpu.VMEM)

    def block(n):
        return pltpu.VMEM((n, PACK, LANES), BF16)

    gq, conv, sums, gks = pl.pallas_call(
        functools.partial(exchange_kernel, sizes),
        out_shape=(
            jax.ShapeDtypeStruct(flat, BF16),
            jax.ShapeDtypeStruct(flat, F32),
            jax.ShapeDtypeStruct((ALL_CHUNKS, PACK, LANES), BF16),
            jax.ShapeDtypeStruct((PACK, LANES), F32),
        ),
        in_specs=[hbm] * 5,
        out_specs=(hbm, hbm, vmem, vmem),
        scratch_shapes=[pltpu.VMEM(flat, BF16)] * 4
        + [
            pltpu.VMEM(kernel.shape, F32),
            pltpu.VMEM((2, tokens // 2, CHANNELS), BF16),
            pltpu.VMEM(flat, F32),
            pltpu.VMEM(flat, F32),
            pltpu.VMEM(flat, BF16),
            block(plane),
            block(line),
            block(STATE_CHUNKS),
            block(plane),
            block(line),
            pltpu.VMEM((STATE_CHUNKS, PACK, LANES), F32),
            block(ALL_CHUNKS),
            block(plane),
            block(line),
            block(ALL_CHUNKS),
            block(plane),
            block(line),
            pltpu.SemaphoreType.DMA((5,)),
            pltpu.SemaphoreType.DMA((2,)),
            pltpu.SemaphoreType.DMA((2,)),
            pltpu.SemaphoreType.DMA((2,)),
            pltpu.SemaphoreType.DMA((10,)),
            pltpu.SemaphoreType.DMA((10,)),
            pltpu.SemaphoreType.REGULAR,
        ],
        compiler_params=pltpu.CompilerParams(
            collective_id=0, has_side_effects=True, vmem_limit_bytes=48 * 1024 * 1024
        ),
    )(q, k, v, g, w)

    gq, gk, gv, gw = pl.pallas_call(
        functools.partial(finish_kernel, count),
        out_shape=(
            jax.ShapeDtypeStruct(flat, BF16),
            jax.ShapeDtypeStruct(flat, BF16),
            jax.ShapeDtypeStruct(flat, BF16),
            jax.ShapeDtypeStruct((3, 3, CHANNELS), F32),
        ),
        in_specs=[hbm] * 4 + [vmem] * 2,
        out_specs=(hbm, hbm, hbm, vmem),
        scratch_shapes=[pltpu.VMEM(flat, BF16)] * 2
        + [pltpu.VMEM(flat, F32)]
        + [pltpu.VMEM(flat, BF16)] * 2
        + [pltpu.SemaphoreType.DMA((3, 3)), pltpu.SemaphoreType.DMA((2, 4))],
        compiler_params=pltpu.CompilerParams(vmem_limit_bytes=48 * 1024 * 1024),
    )(k, v, conv, gq, sums, gks)
    return gq.reshape(shape), gk.reshape(shape), gv.reshape(shape), gw


def solution(mesh):
    sizes = (mesh.shape["tm"], mesh.shape["rows"])
    placed = P("tm", "rows", None, None)
    return jax.shard_map(
        functools.partial(shards, sizes),
        mesh=mesh,
        in_specs=(placed, placed, placed, placed, P()),
        out_specs=(placed, placed, placed, P()),
        check_vma=False,
    )
```

time: 752 us -> 54.3 us (0.07)
  waiting for transfers between devices: 454 us -> 0 us
  blocking collectives: 211 us -> 0 us
  Pallas kernels: 0 us -> 53.5 us
  local copies, waits for them, and re-layouts: 32.1 us -> 0 us
  other arithmetic: 14.8 us -> 0 us
  between operations: 14.5 us -> 0.64 us
  matrix products: 13.3 us -> 0 us
  starting transfers between devices: 11 us -> 0 us
    psum x1 -> x0, waiting for transfers between devices: 454 us -> none  [shards(): states, keysum = lax.psum((part_states, part_keysum), ('tm', 'rows'))]
    psum x2 -> x0, blocking collectives: 211 us -> none  [the longest x1 106 us: shards(): states, keysum = lax.psum((part_states, part_keysum), ('tm', 'rows'))]
    pallas_call x0 -> x2, Pallas kernels: none -> 53.5 us  [the longest x1 50 us: shards(): pl.pallas_call(functools.partial(exchange_kernel, sizes), out_shape=(jax....]
    dot_general x8 -> x0, matrix products: 13.3 us -> none  [the longest x1 3.07 us: shards(): part_gstate = jnp.einsum('nhe,nhf->hef', pos_qf, dnum, precision=HIGH)]
    ppermute x2 -> x0, starting transfers between devices: 11 us -> none  [the longest x1 5.94 us: padded_2(): after = lax.ppermute(leading, axis, down)]
    max x4 -> x0, local copies, waits for them, and re-layouts: 7.63 us -> none  [the longest x2 5.05 us: shards(): pos_q = jnp.maximum(q_flat, 0)]
  transfers between devices with their start and end apart: 3 -> 0, of which waited for: 1 -> 0; matrix products, arithmetic and copies ran while one was open for 6% -> 0% of each run, Pallas kernels for 0% -> 0%
where the time goes in v1:
time: 54.3 us; the launch traced here: 54.2 us
  Pallas kernels  53.5 us (99%)
  between operations  0.64 us (1%)
    pallas_call x1, Pallas kernels, shards(): pl.pallas_call(functools.partial(exchange_kernel, sizes), out_shape=(jax....  50 us
    pallas_call x1, Pallas kernels, shards(): pl.pallas_call(functools.partial(finish_kernel, count), out_shape=(jax.Sh...  3.56 us

profile of v1, /device:TPU:1, one launch (start us, length us, event | category | flops | bytes accessed | tf_op | source)
XLA Modules:
  0.0 54.2 jit_solution(10884559840381308366)
XLA Ops:
  0.6 50.0 %shard_map.84 = (bf16[256,1152]{1,0:T(8,128)(2,1)S(1)}, f32[256,1152]{1,0:T(8,128)S(1)}, bf16[27,16,128]{2,1,0:T(8,128)(2,1)S(1)}, f32[16,128]{1,0:T(8,128)S(1)}) custom-call(bf16[256,1152]{1,0:T(8,128)(2,1)} %bitcast.11, bf16[256,1152]{1,0:T(8,128)(2,1)} %bitcast.7, bf16[256,1152]{1,0:T(8,128)(2,1)} %bitcast.9, bf16[256,1152]{1,0:T(8,128)(2,1)} %bitcast.12, ...), custom_call_target="tpu_custom_call" | custom-call | tf_op jit(solution)/shard_map/pallas_call | solution.py:504
  50.6 3.6 %shard_map.85 = (bf16[256,1152]{1,0:T(8,128)(2,1)}, bf16[256,1152]{1,0:T(8,128)(2,1)}, bf16[256,1152]{1,0:T(8,128)(2,1)}, f32[3,3,1152]{2,1,0:T(4,128)}) custom-call(bf16[256,1152]{1,0:T(8,128)(2,1)} %bitcast.8, bf16[256,1152]{1,0:T(8,128)(2,1)} %bitcast.10, f32[256,1152]{1,0:T(8,128)S(1)} %get-tuple-element.12.conv_hbm, ...), custom_call_target="tpu_custom_call" | custom-call | tf_op jit(solution)/shard_map/pallas_call | solution.py:546

commit v2 on v1

v2 whole, which is shorter than its diff:
```python
import functools

import jax
import jax.numpy as jnp
from jax import lax
from jax.experimental import pallas as pl
from jax.experimental.pallas import tpu as pltpu
from jax.sharding import PartitionSpec as P

MESH = pl.DeviceIdType.MESH
F32 = jnp.float32
BF16 = jnp.bfloat16

HEADS = 36
HEAD_DIM = 32
DEN_EPS = 0.1

LANES = 128
CHANNELS = HEADS * HEAD_DIM
GROUPS = CHANNELS // LANES
PACK = 16
STATE_CHUNKS = GROUPS * HEAD_DIM // PACK


def lanes(group):
    return pl.ds(group * LANES, LANES)


def block_mask():
    row = lax.broadcasted_iota(jnp.int32, (LANES, LANES), 0)
    col = lax.broadcasted_iota(jnp.int32, (LANES, LANES), 1)
    return (row // HEAD_DIM) == (col // HEAD_DIM)


def pack_heads(full):
    col = lax.broadcasted_iota(jnp.int32, (HEAD_DIM, LANES), 1) // HEAD_DIM
    out = full[0:HEAD_DIM]
    for h in range(1, LANES // HEAD_DIM):
        out = jnp.where(col == h, full[h * HEAD_DIM : (h + 1) * HEAD_DIM], out)
    return out


def unpack_heads(packed, mask):
    tiled = jnp.concatenate([packed.astype(F32)] * (LANES // HEAD_DIM), axis=0)
    return jnp.where(mask, tiled, 0.0)


def split(x):
    high = x.astype(BF16)
    return jnp.concatenate([high, (x - high.astype(F32)).astype(BF16)], axis=1)


def total(slots):
    return jnp.sum(slots.astype(F32), axis=0)


def farthest_first(sizes):
    offsets = [()]
    for size in sizes:
        offsets = [o + (d,) for o in offsets for d in range(size)]
    hops = lambda o: sum(min(d, n - d) for d, n in zip(o, sizes))
    return sorted((o for o in offsets if any(o)), key=hops, reverse=True)


SIDE = 4
PLANE = 2 * SIDE * SIDE
STATE_OWNERS = 0
GRAD_OWNERS = PLANE - STATE_CHUNKS
TAP_OWNERS = 0


def exchange_kernel(
    sizes,
    q_hbm,
    k_hbm,
    v_hbm,
    g_hbm,
    w_hbm,
    gq,
    gv,
    dk,
    gw,
    kb,
    gks_out,
    conv,
    vb,
    qb,
    gb,
    w_ref,
    pq_turned,
    halo,
    inv_den,
    weight,
    ks_plane,
    ks_line,
    st_src,
    st_rs,
    st_line,
    st_all,
    st_low,
    gs_src,
    gs_rs,
    gs_line,
    gs_all,
    wk_src,
    wk_rs,
    wk_line,
    wk_all,
    gk_plane,
    gk_line,
    load_sem,
    halo_send,
    halo_recv,
    send_sem,
    recv_sem,
    relay_sem,
):
    tm_size, rows_size = sizes
    line_size = rows_size // 2
    tokens = kb.shape[0]
    count = tokens * tm_size * rows_size
    width = tokens // 2
    tm = lax.axis_index("tm")
    r = lax.axis_index("rows")
    z, core = lax.div(r, 2), lax.rem(r, 2)
    x, y = lax.div(tm, SIDE), lax.rem(tm, SIDE)
    me = core * tm_size + tm

    loads = [
        pltpu.make_async_copy(src, dst, load_sem.at[i])
        for i, (src, dst) in enumerate(
            ((k_hbm, kb), (v_hbm, vb), (q_hbm, qb), (g_hbm, gb), (w_hbm, w_ref))
        )
    ]
    loads[0].start()

    xs = [lax.rem(x + d, SIDE) * SIDE for d in range(SIDE)]
    ys = [lax.rem(y + d, SIDE) for d in range(SIDE)]
    cs = [core, 1 - core]
    plane = []
    for dx, dy, dc in farthest_first((SIDE, SIDE, 2)):
        chip = xs[dx] + ys[dy]
        plane.append((cs[dc] * tm_size + chip, (chip, 2 * z + cs[dc])))
    line = []
    for (d,) in farthest_first((line_size,)):
        line.append((tm, 2 * lax.rem(z + d, line_size) + core))
    near = line_size // 4
    barrier = pltpu.get_barrier_semaphore()

    def greet(device):
        pl.semaphore_signal(barrier, inc=1, device_id=device, device_id_type=MESH)

    def line_at(d):
        return (tm, 2 * lax.rem(z + d + line_size, line_size) + core)

    for _, device in plane:
        greet(device)
    for d in range(near, 0, -1):
        greet(line_at(d))
        greet(line_at(-d))
    greet((tm, lax.rem(r + 2 * core + rows_size - 1, rows_size)))
    for load in loads[1:]:
        load.start()

    def remote(src, dst, which, device):
        return pltpu.make_async_remote_copy(
            src_ref=src,
            dst_ref=dst,
            send_sem=send_sem.at[which],
            recv_sem=recv_sem.at[which],
            device_id=device,
            device_id_type=MESH,
        )

    def to_plane(buf, slot, which):
        for _, device in plane:
            remote(buf.at[slot], buf.at[slot], which, device).start()

    def to_line(buf, which):
        for device in line:
            remote(buf.at[z], buf.at[z], which, device).start()

    def owned(first, chunks):
        return jnp.logical_and(me >= first, me < first + chunks)

    def to_owners(src, dst, first, chunks, which):
        for index, device in plane:

            @pl.when(jnp.logical_and(index >= first, index < first + chunks))
            def _(index=index, device=device):
                remote(src.at[index - first], dst.at[me], which, device).start()

        @pl.when(owned(first, chunks))
        def _():
            dst[me] = src[me - first]

    def to_owner(src, dst, first, chunk, which):
        index = first + chunk

        @pl.when(me != index)
        def _():
            device = (index % tm_size, 2 * z + index // tm_size)
            remote(src.at[chunk], dst.at[me], which, device).start()

        @pl.when(me == index)
        def _():
            dst[me] = src[chunk]

    def arrived(buf, n, sem):
        view = buf.at[pl.ds(0, n)]
        pltpu.make_async_copy(view, view, sem).wait()

    def all_arrived(buf, first, chunks, sem):
        @pl.when(owned(first, chunks))
        def _():
            arrived(buf, chunks - 1, sem)

        @pl.when(jnp.logical_not(owned(first, chunks)))
        def _():
            arrived(buf, chunks, sem)

    KS1, KS2, ST1, ST2, ST3, ST4, GS1, GS2, GS3, WK1, WK2, WK3, GK1, GK2 = range(14)
    mask = block_mask()
    ones_block = jnp.where(mask, 1.0, 0.0).astype(BF16)
    ones_twice = jnp.concatenate([ones_block, ones_block], axis=0)
    row16 = lax.broadcasted_iota(jnp.int32, (PACK, LANES), 0)
    groups = [slice(i * LANES, (i + 1) * LANES) for i in range(GROUPS)]

    loads[0].wait()
    ks_rows = jnp.zeros((PACK, LANES), F32)
    ones = jnp.ones((PACK, tokens), BF16)
    for i, at in enumerate(groups):
        ks = jnp.dot(ones, jnp.maximum(kb[:, at], 0), preferred_element_type=F32)
        ks_rows = jnp.where(row16 == i, ks, ks_rows)
    ks_plane[me] = ks_rows.astype(BF16)
    loads[1].wait()
    for i, at in enumerate(groups):
        full = lax.dot_general(
            jnp.maximum(kb[:, at], 0),
            vb[:, at],
            (((0,), (0,)), ((), ())),
            preferred_element_type=F32,
        )
        st_src[2 * i : 2 * i + 2] = pack_heads(full).astype(BF16).reshape(2, PACK, LANES)

    pl.semaphore_wait(barrier, len(plane) + 2 * near + 1)
    to_plane(ks_plane, me, KS1)
    to_owners(st_src, st_rs, STATE_OWNERS, STATE_CHUNKS, ST1)
    for d in (near, -near):
        pl.semaphore_signal(relay_sem, inc=1, device_id=line_at(d), device_id_type=MESH)

    loads[3].wait()

    def to_before():
        return pltpu.make_async_remote_copy(
            src_ref=gb.at[pl.ds(0, width)],
            dst_ref=halo.at[1],
            send_sem=halo_send.at[0],
            recv_sem=halo_recv.at[1],
            device_id=(tm, r - 1),
            device_id_type=MESH,
        )

    def to_after():
        return pltpu.make_async_remote_copy(
            src_ref=gb.at[pl.ds(width, width)],
            dst_ref=halo.at[0],
            send_sem=halo_send.at[1],
            recv_sem=halo_recv.at[0],
            device_id=(tm, r + 1),
            device_id_type=MESH,
        )

    @pl.when(r > 0)
    def _():
        to_before().start()

    @pl.when(r == 0)
    def _():
        halo[0] = jnp.zeros(halo.shape[1:], BF16)

    @pl.when(r < rows_size - 1)
    def _():
        to_after().start()

    @pl.when(r == rows_size - 1)
    def _():
        halo[1] = jnp.zeros(halo.shape[1:], BF16)

    loads[2].wait()
    for at in groups:
        pq_turned[at, :] = jnp.maximum(qb[:, at], 0).T

    arrived(ks_plane, PLANE - 1, recv_sem.at[KS1])
    ks_line[z] = total(ks_plane[...]).astype(BF16)
    pl.semaphore_wait(relay_sem, 2)
    to_line(ks_line, KS2)

    @pl.when(owned(STATE_OWNERS, STATE_CHUNKS))
    def _():
        arrived(st_rs, PLANE - 1, recv_sem.at[ST1])
        st_line[z] = total(st_rs[...]).astype(BF16)
        to_line(st_line, ST2)

    @pl.when(r > 0)
    def _():
        pltpu.make_async_copy(halo.at[0], halo.at[0], halo_recv.at[0]).wait()

    @pl.when(r < rows_size - 1)
    def _():
        pltpu.make_async_copy(halo.at[1], halo.at[1], halo_recv.at[1]).wait()

    loads[4].wait()

    def conv_group(i, _):
        at = pl.ds(pl.multiple_of(i * LANES, LANES), LANES)
        col = lax.broadcasted_iota(jnp.int32, (width, LANES), 0)
        grads = (halo[0, :, at], gb[0:width, at], gb[width:, at], halo[1, :, at])
        vals = [vb[0:width, at].astype(F32), vb[width:, at].astype(F32)]
        out = [jnp.zeros((width, LANES), F32) for _ in range(2)]
        taps = [jnp.zeros((8, LANES), F32) for _ in range(9)]
        for s in range(4):
            base = grads[s].astype(F32)
            for b in (-1, 0, 1):
                if b == 1:
                    moved = jnp.where(col == 0, 0.0, pltpu.roll(base, 1, 0))
                elif b == -1:
                    moved = jnp.where(col == width - 1, 0.0, pltpu.roll(base, width - 1, 0))
                else:
                    moved = base
                for j in range(2):
                    a = j + 1 - s
                    if -1 <= a <= 1:
                        tap = (a + 1) * 3 + b + 1
                        out[j] = out[j] + w_ref[a + 1, b + 1 : b + 2, at] * moved
                        product = (vals[j] * moved).reshape(width // 8, 8, LANES)
                        taps[tap] = taps[tap] + jnp.sum(product, axis=0)
        conv[0:width, at] = out[0]
        conv[width:, at] = out[1]
        rows = jnp.zeros((PACK, LANES), F32)
        for tap in range(9):
            rows = jnp.where(row16 == tap, jnp.sum(taps[tap], axis=0, keepdims=True), rows)
        wk_src[i] = rows.astype(BF16)
        return 0

    lax.fori_loop(0, GROUPS, conv_group, 0)
    to_owners(wk_src, wk_rs, TAP_OWNERS, GROUPS, WK1)

    arrived(ks_line, line_size - 1, recv_sem.at[KS2])
    keysum = total(ks_line[...]) * (1.0 / count)
    for i, at in enumerate(groups):
        pq = jnp.maximum(qb[:, at], 0).astype(F32)
        weighted = split(pq * keysum[i : i + 1])
        den = jnp.dot(weighted, ones_twice, preferred_element_type=F32) + DEN_EPS
        inv = pl.reciprocal(den, approx=True)
        inv = inv * (2.0 - den * inv)
        inv_den[:, at] = inv
        dnum = (gb[:, at].astype(F32) * inv).astype(BF16)
        full = jnp.dot(pq_turned[at, :], dnum, preferred_element_type=F32)
        gs_src[2 * i : 2 * i + 2] = pack_heads(full).astype(BF16).reshape(2, PACK, LANES)
        for chunk in (2 * i, 2 * i + 1):
            to_owner(gs_src, gs_rs, GRAD_OWNERS, chunk, GS1)

    @pl.when(owned(STATE_OWNERS, STATE_CHUNKS))
    def _():
        arrived(st_line, line_size - 1, recv_sem.at[ST2])
        chunk = me - STATE_OWNERS
        state = total(st_line[...]) * (1.0 / count)
        high = state.astype(BF16)
        st_all[chunk] = high
        to_plane(st_all, chunk, ST3)
        st_low[chunk] = (state - high.astype(F32)).astype(BF16)

    for at in groups:
        inv = inv_den[:, at]
        weight[:, at] = jnp.maximum(qb[:, at].astype(F32), 0.0) * (inv * inv)

    @pl.when(owned(TAP_OWNERS, GROUPS))
    def _():
        arrived(wk_rs, PLANE - 1, recv_sem.at[WK1])
        wk_line[z] = total(wk_rs[...]).astype(BF16)
        to_line(wk_line, WK2)

    @pl.when(owned(GRAD_OWNERS, STATE_CHUNKS))
    def _():
        arrived(gs_rs, PLANE - 1, recv_sem.at[GS1])
        gs_line[z] = total(gs_rs[...]).astype(BF16)
        to_line(gs_line, GS2)

    all_arrived(st_all, STATE_OWNERS, STATE_CHUNKS, recv_sem.at[ST3])
    gk_rows = jnp.zeros((PACK, LANES), F32)
    for i, at in enumerate(groups):
        state = unpack_heads(st_all[2 * i : 2 * i + 2].reshape(HEAD_DIM, LANES), mask)
        pulled = lax.dot_general(
            gb[:, at], state.astype(BF16), (((1,), (1,)), ((), ())), preferred_element_type=F32
        )
        pq = jnp.maximum(qb[:, at].astype(F32), 0.0)
        inner = jnp.dot((pq * pulled).astype(BF16), ones_block, preferred_element_type=F32)
        part = jnp.sum(weight[:, at] * inner, axis=0, keepdims=True)
        gk_rows = jnp.where(row16 == i, -part, gk_rows)
    gk_plane[me] = gk_rows.astype(BF16)
    to_plane(gk_plane, me, GK1)

    @pl.when(owned(STATE_OWNERS, STATE_CHUNKS))
    def _():
        to_plane(st_low, me - STATE_OWNERS, ST4)

    @pl.when(owned(TAP_OWNERS, GROUPS))
    def _():
        arrived(wk_line, line_size - 1, recv_sem.at[WK2])
        chunk = me - TAP_OWNERS
        wk_all[chunk] = total(wk_line[...]).astype(BF16)
        to_plane(wk_all, chunk, WK3)

    arrived(gk_plane, PLANE - 1, recv_sem.at[GK1])
    gk_line[z] = total(gk_plane[...]).astype(BF16)
    to_line(gk_line, GK2)

    @pl.when(owned(GRAD_OWNERS, STATE_CHUNKS))
    def _():
        arrived(gs_line, line_size - 1, recv_sem.at[GS2])
        chunk = me - GRAD_OWNERS
        gs_all[chunk] = (total(gs_line[...]) * (1.0 / count)).astype(BF16)
        to_plane(gs_all, chunk, GS3)

    all_arrived(st_low, STATE_OWNERS, STATE_CHUNKS, recv_sem.at[ST4])
    for i, at in enumerate(groups):
        state = jnp.concatenate(
            [
                unpack_heads(half[2 * i : 2 * i + 2].reshape(HEAD_DIM, LANES), mask).astype(BF16)
                for half in (st_all, st_low)
            ],
            axis=1,
        )
        grad = gb[:, at]
        pulled = lax.dot_general(
            jnp.concatenate([grad, grad], axis=1),
            state,
            (((1,), (1,)), ((), ())),
            preferred_element_type=F32,
        )
        pq = jnp.maximum(qb[:, at].astype(F32), 0.0)
        inner = jnp.dot(split(pq * pulled), ones_twice, preferred_element_type=F32)
        inv = inv_den[:, at]
        dq = (pulled - inner * (inv * keysum[i : i + 1])) * inv
        gq[:, at] = jnp.where(pq > 0, dq, 0.0).astype(BF16)

    @pl.when(r > 0)
    def _():
        to_before().wait_send()

    @pl.when(r < rows_size - 1)
    def _():
        to_after().wait_send()

    for buf, which in ((ks_plane, KS1), (gk_plane, GK1)):
        arrived(buf, PLANE - 1, send_sem.at[which])
    for buf, which in ((ks_line, KS2), (gk_line, GK2)):
        arrived(buf, line_size - 1, send_sem.at[which])
    for first, chunks, src, rs, lined, steps in (
        (STATE_OWNERS, STATE_CHUNKS, st_src, st_rs, st_line, (ST1, ST2, ST3, ST4)),
        (GRAD_OWNERS, STATE_CHUNKS, gs_src, gs_rs, gs_line, (GS1, GS2, GS3)),
        (TAP_OWNERS, GROUPS, wk_src, wk_rs, wk_line, (WK1, WK2, WK3)),
    ):
        all_arrived(src, first, chunks, send_sem.at[steps[0]])

        @pl.when(owned(first, chunks))
        def _(rs=rs, lined=lined, steps=steps):
            arrived(lined, line_size - 1, send_sem.at[steps[1]])
            for step in steps[2:]:
                arrived(rs, PLANE - 1, send_sem.at[step])

    all_arrived(wk_all, TAP_OWNERS, GROUPS, recv_sem.at[WK3])
    for i, at in enumerate(groups):
        rows = wk_all[i].astype(F32)
        for a in range(3):
            gw[a, :, at] = rows[3 * a : 3 * a + 3]

    all_arrived(gs_all, GRAD_OWNERS, STATE_CHUNKS, recv_sem.at[GS3])
    for i, at in enumerate(groups):
        grad = unpack_heads(gs_all[2 * i : 2 * i + 2].reshape(HEAD_DIM, LANES), mask)
        grad = grad.astype(BF16)
        dk[:, at] = lax.dot_general(
            vb[:, at], grad, (((1,), (1,)), ((), ())), preferred_element_type=F32
        )
        dv = jnp.dot(jnp.maximum(kb[:, at], 0), grad, preferred_element_type=F32)
        gv[:, at] = (dv + conv[:, at]).astype(BF16)
    arrived(gk_line, line_size - 1, recv_sem.at[GK2])
    gks_out[...] = total(gk_line[...]) * (1.0 / count)


def finish_kernel(
    gq, gv, dk, gw, kb, gks, gq_out, gk_out, gv_out, gw_out, gk, pass_sem, store_sem
):
    stores = [
        pltpu.make_async_copy(src, dst, pass_sem.at[i])
        for i, (src, dst) in enumerate(((gq, gq_out), (gv, gv_out), (gw, gw_out)))
    ]
    for store in stores:
        store.start()
    parts = 3
    wide = CHANNELS // parts
    for p in range(parts):
        for i in range(p * (GROUPS // parts), (p + 1) * (GROUPS // parts)):
            at = slice(i * LANES, (i + 1) * LANES)
            value = dk[:, at] + gks[i : i + 1]
            gk[:, at] = jnp.where(kb[:, at].astype(F32) > 0, value, 0.0).astype(BF16)
        at = pl.ds(p * wide, wide)
        store = pltpu.make_async_copy(gk.at[:, at], gk_out.at[:, at], store_sem.at[p])
        store.start()
        stores.append(store)
    for store in stores:
        store.wait()


def shards(sizes, queries, keys, values, cotangent, kernel):
    shape = queries.shape
    tokens = shape[0] * shape[1] * shape[2]
    flat = (tokens, CHANNELS)
    line = sizes[1] // 2
    q, k, v, g = (x.reshape(flat) for x in (queries, keys, values, cotangent))
    q, k, v, g, w = (
        pltpu.with_memory_space_constraint(x, pltpu.HBM) for x in (q, k, v, g, kernel)
    )
    hbm = pl.BlockSpec(memory_space=pltpu.HBM)
    vmem = pl.BlockSpec(memory_space=pltpu.VMEM)

    def block(n):
        return pltpu.VMEM((n, PACK, LANES), BF16)

    def chain(chunks):
        return [block(chunks), block(PLANE), block(line), block(chunks)]

    gq, gv, dk, gw, kb, gks = pl.pallas_call(
        functools.partial(exchange_kernel, sizes),
        out_shape=(
            jax.ShapeDtypeStruct(flat, BF16),
            jax.ShapeDtypeStruct(flat, BF16),
            jax.ShapeDtypeStruct(flat, F32),
            jax.ShapeDtypeStruct(kernel.shape, F32),
            jax.ShapeDtypeStruct(flat, BF16),
            jax.ShapeDtypeStruct((PACK, LANES), F32),
        ),
        in_specs=[hbm] * 5,
        out_specs=(vmem,) * 6,
        scratch_shapes=[pltpu.VMEM(flat, F32)]
        + [pltpu.VMEM(flat, BF16)] * 3
        + [
            pltpu.VMEM(kernel.shape, F32),
            pltpu.VMEM((CHANNELS, tokens), BF16),
            pltpu.VMEM((2, tokens // 2, CHANNELS), BF16),
            pltpu.VMEM(flat, F32),
            pltpu.VMEM(flat, F32),
            block(PLANE),
            block(line),
        ]
        + chain(STATE_CHUNKS)
        + [block(STATE_CHUNKS)]
        + chain(STATE_CHUNKS)
        + chain(GROUPS)
        + [
            block(PLANE),
            block(line),
            pltpu.SemaphoreType.DMA((5,)),
            pltpu.SemaphoreType.DMA((2,)),
            pltpu.SemaphoreType.DMA((2,)),
            pltpu.SemaphoreType.DMA((14,)),
            pltpu.SemaphoreType.DMA((14,)),
            pltpu.SemaphoreType.REGULAR,
        ],
        compiler_params=pltpu.CompilerParams(
            collective_id=0, has_side_effects=True, vmem_limit_bytes=32 * 1024 * 1024
        ),
    )(q, k, v, g, w)

    gq, gk, gv, gw = pl.pallas_call(
        finish_kernel,
        out_shape=(
            jax.ShapeDtypeStruct(flat, BF16),
            jax.ShapeDtypeStruct(flat, BF16),
            jax.ShapeDtypeStruct(flat, BF16),
            jax.ShapeDtypeStruct((3, 3, CHANNELS), F32),
        ),
        in_specs=[vmem] * 6,
        out_specs=(hbm,) * 4,
        scratch_shapes=[
            pltpu.VMEM(flat, BF16),
            pltpu.SemaphoreType.DMA((3,)),
            pltpu.SemaphoreType.DMA((3,)),
        ],
        compiler_params=pltpu.CompilerParams(vmem_limit_bytes=32 * 1024 * 1024),
    )(gq, gv, dk, gw, kb, gks)
    return gq.reshape(shape), gk.reshape(shape), gv.reshape(shape), gw


def solution(mesh):
    sizes = (mesh.shape["tm"], mesh.shape["rows"])
    placed = P("tm", "rows", None, None)
    return jax.shard_map(
        functools.partial(shards, sizes),
        mesh=mesh,
        in_specs=(placed, placed, placed, placed, P()),
        out_specs=(placed, placed, placed, P()),
        check_vma=False,
    )
```

time: 54.3 us -> 50.4 us (0.928)
  Pallas kernels: 53.5 us -> 49.6 us
    pallas_call x1, Pallas kernels: 3.56 us -> 1.27 us  [shards(): pl.pallas_call(finish_kernel, out_shape=(jax.ShapeDtypeStruct(flat, BF16)...]
    pallas_call x1, Pallas kernels: 50 us -> 48.3 us  [shards(): pl.pallas_call(functools.partial(exchange_kernel, sizes), out_shape=(jax....]
where the time goes in v2:
time: 50.4 us; the launch traced here: 50.2 us
  Pallas kernels  49.6 us (98%)
  between operations  0.64 us (1%)
    pallas_call x1, Pallas kernels, shards(): pl.pallas_call(functools.partial(exchange_kernel, sizes), out_shape=(jax....  48.3 us
    pallas_call x1, Pallas kernels, shards(): pl.pallas_call(finish_kernel, out_shape=(jax.ShapeDtypeStruct(flat, BF16)...  1.27 us

profile of v2, /device:TPU:1, one launch (start us, length us, event | category | flops | bytes accessed | tf_op | source)
XLA Modules:
  0.0 50.2 jit_solution(14999680509654618721)
XLA Ops:
  0.6 48.3 %shard_map.84 = (bf16[256,1152]{1,0:T(8,128)(2,1)S(1)}, bf16[256,1152]{1,0:T(8,128)(2,1)S(1)}, f32[256,1152]{1,0:T(8,128)S(1)}, f32[3,3,1152]{2,1,0:T(4,128)S(1)...) custom-call(bf16[256,1152]{1,0:T(8,128)(2,1)} %bitcast.7, bf16[256,1152]{1,0:T(8,128)(2,1)} %bitcast.8, ...), custom_call_target="tpu_custom_call" | custom-call | tf_op jit(solution)/shard_map/pallas_call | solution.py:534
  48.9 1.3 %shard_map.85 = (bf16[256,1152]{1,0:T(8,128)(2,1)}, bf16[256,1152]{1,0:T(8,128)(2,1)}, bf16[256,1152]{1,0:T(8,128)(2,1)}, f32[3,3,1152]{2,1,0:T(4,128)}) custom-call(bf16[256,1152]{1,0:T(8,128)(2,1)S(1)} %get-tuple-element.14.gq, bf16[256,1152]{1,0:T(8,128)(2,1)S(1)} %get-tuple-element.15.gv, f32[256,1152]{1,0:T(8,128)S(1)} %get-tuple-element.16.dk, ...), custom_call_target="tpu_custom_call" | custom-call | tf_op jit(solution)/shard_map/pallas_call | solution.py:576

commit v3 on v2

--- a/solution.py
+++ b/solution.py
@@ -183,28 +183,27 @@
     def owned(first, chunks):
         return jnp.logical_and(me >= first, me < first + chunks)
 
-    def to_owners(src, dst, first, chunks, which):
-        for index, device in plane:
-
-            @pl.when(jnp.logical_and(index >= first, index < first + chunks))
-            def _(index=index, device=device):
-                remote(src.at[index - first], dst.at[me], which, device).start()
-
-        @pl.when(owned(first, chunks))
+    def to_owners(src, dst, first, begin, end, which):
+        n = end - begin
+        mine = lax.rem(me - first - begin + PLANE, PLANE)
+        start = lax.rem(mine, n)
+
+        def send(i):
+            chunk = begin + lax.rem(start + i, n)
+            index = first + chunk
+            device = (lax.rem(index, tm_size), 2 * z + lax.div(index, tm_size))
+            remote(src.at[chunk], dst.at[me], which, device).start()
+
+        for i in range(1, n):
+            send(i)
+
+        @pl.when(mine < n)
         def _():
-            dst[me] = src[me - first]
-
-    def to_owner(src, dst, first, chunk, which):
-        index = first + chunk
-
-        @pl.when(me != index)
+            dst[me] = src[begin + start]
+
+        @pl.when(mine >= n)
         def _():
-            device = (index % tm_size, 2 * z + index // tm_size)
-            remote(src.at[chunk], dst.at[me], which, device).start()
-
-        @pl.when(me == index)
-        def _():
-            dst[me] = src[chunk]
+            send(0)
 
     def arrived(buf, n, sem):
         view = buf.at[pl.ds(0, n)]
@@ -244,10 +243,10 @@
         st_src[2 * i : 2 * i + 2] = pack_heads(full).astype(BF16).reshape(2, PACK, LANES)
 
     pl.semaphore_wait(barrier, len(plane) + 2 * near + 1)
-    to_plane(ks_plane, me, KS1)
-    to_owners(st_src, st_rs, STATE_OWNERS, STATE_CHUNKS, ST1)
     for d in (near, -near):
         pl.semaphore_signal(relay_sem, inc=1, device_id=line_at(d), device_id_type=MESH)
+    to_plane(ks_plane, me, KS1)
+    to_owners(st_src, st_rs, STATE_OWNERS, 0, STATE_CHUNKS, ST1)
 
     loads[3].wait()
 
@@ -344,7 +343,7 @@
         return 0
 
     lax.fori_loop(0, GROUPS, conv_group, 0)
-    to_owners(wk_src, wk_rs, TAP_OWNERS, GROUPS, WK1)
+    to_owners(wk_src, wk_rs, TAP_OWNERS, 0, GROUPS, WK1)
 
     arrived(ks_line, line_size - 1, recv_sem.at[KS2])
     keysum = total(ks_line[...]) * (1.0 / count)
@@ -358,8 +357,8 @@
         dnum = (gb[:, at].astype(F32) * inv).astype(BF16)
         full = jnp.dot(pq_turned[at, :], dnum, preferred_element_type=F32)
         gs_src[2 * i : 2 * i + 2] = pack_heads(full).astype(BF16).reshape(2, PACK, LANES)
-        for chunk in (2 * i, 2 * i + 1):
-            to_owner(gs_src, gs_rs, GRAD_OWNERS, chunk, GS1)
+        if i % 3 == 2:
+            to_owners(gs_src, gs_rs, GRAD_OWNERS, 2 * i - 4, 2 * i + 2, GS1)
 
     @pl.when(owned(STATE_OWNERS, STATE_CHUNKS))
     def _():
@@ -381,6 +380,10 @@
         wk_line[z] = total(wk_rs[...]).astype(BF16)
         to_line(wk_line, WK2)
 
+    @pl.when(owned(STATE_OWNERS, STATE_CHUNKS))
+    def _():
+        to_plane(st_low, me - STATE_OWNERS, ST4)
+
     @pl.when(owned(GRAD_OWNERS, STATE_CHUNKS))
     def _():
         arrived(gs_rs, PLANE - 1, recv_sem.at[GS1])
@@ -400,28 +403,6 @@
         gk_rows = jnp.where(row16 == i, -part, gk_rows)
     gk_plane[me] = gk_rows.astype(BF16)
     to_plane(gk_plane, me, GK1)
-
-    @pl.when(owned(STATE_OWNERS, STATE_CHUNKS))
-    def _():
-        to_plane(st_low, me - STATE_OWNERS, ST4)
-
-    @pl.when(owned(TAP_OWNERS, GROUPS))
-    def _():
-        arrived(wk_line, line_size - 1, recv_sem.at[WK2])
-        chunk = me - TAP_OWNERS
-        wk_all[chunk] = total(wk_line[...]).astype(BF16)
-        to_plane(wk_all, chunk, WK3)
-
-    arrived(gk_plane, PLANE - 1, recv_sem.at[GK1])
-    gk_line[z] = total(gk_plane[...]).astype(BF16)
-    to_line(gk_line, GK2)
-
-    @pl.when(owned(GRAD_OWNERS, STATE_CHUNKS))
-    def _():
-        arrived(gs_line, line_size - 1, recv_sem.at[GS2])
-        chunk = me - GRAD_OWNERS
-        gs_all[chunk] = (total(gs_line[...]) * (1.0 / count)).astype(BF16)
-        to_plane(gs_all, chunk, GS3)
 
     all_arrived(st_low, STATE_OWNERS, STATE_CHUNKS, recv_sem.at[ST4])
     for i, at in enumerate(groups):
@@ -444,6 +425,24 @@
         inv = inv_den[:, at]
         dq = (pulled - inner * (inv * keysum[i : i + 1])) * inv
         gq[:, at] = jnp.where(pq > 0, dq, 0.0).astype(BF16)
+
+    @pl.when(owned(TAP_OWNERS, GROUPS))
+    def _():
+        arrived(wk_line, line_size - 1, recv_sem.at[WK2])
+        chunk = me - TAP_OWNERS
+        wk_all[chunk] = total(wk_line[...]).astype(BF16)
+        to_plane(wk_all, chunk, WK3)
+
+    arrived(gk_plane, PLANE - 1, recv_sem.at[GK1])
+    gk_line[z] = total(gk_plane[...]).astype(BF16)
+    to_line(gk_line, GK2)
+
+    @pl.when(owned(GRAD_OWNERS, STATE_CHUNKS))
+    def _():
+        arrived(gs_line, line_size - 1, recv_sem.at[GS2])
+        chunk = me - GRAD_OWNERS
+        gs_all[chunk] = (total(gs_line[...]) * (1.0 / count)).astype(BF16)
+        to_plane(gs_all, chunk, GS3)
 
     @pl.when(r > 0)
     def _():

time: 50.4 us -> 49.8 us (0.988)
    pallas_call x1, Pallas kernels: 48.3 us -> 47.8 us  [shards(): pl.pallas_call(functools.partial(exchange_kernel, sizes), out_shape=(jax....]
where the time goes in v3:
time: 49.8 us; the launch traced here: 49.7 us
  Pallas kernels  49.1 us (99%)
  between operations  0.64 us (1%)
    pallas_call x1, Pallas kernels, shards(): pl.pallas_call(functools.partial(exchange_kernel, sizes), out_shape=(jax....  47.8 us
    pallas_call x1, Pallas kernels, shards(): pl.pallas_call(finish_kernel, out_shape=(jax.ShapeDtypeStruct(flat, BF16)...  1.27 us

profile of v3, /device:TPU:1, one launch (start us, length us, event | category | flops | bytes accessed | tf_op | source)
XLA Modules:
  0.0 49.7 jit_solution(13745904340605986231)
XLA Ops:
  0.6 47.8 %shard_map.84 = (bf16[256,1152]{1,0:T(8,128)(2,1)S(1)}, bf16[256,1152]{1,0:T(8,128)(2,1)S(1)}, f32[256,1152]{1,0:T(8,128)S(1)}, f32[3,3,1152]{2,1,0:T(4,128)S(1)...) custom-call(bf16[256,1152]{1,0:T(8,128)(2,1)} %bitcast.7, bf16[256,1152]{1,0:T(8,128)(2,1)} %bitcast.8, ...), custom_call_target="tpu_custom_call" | custom-call | tf_op jit(solution)/shard_map/pallas_call | solution.py:533
  48.4 1.3 %shard_map.85 = (bf16[256,1152]{1,0:T(8,128)(2,1)}, bf16[256,1152]{1,0:T(8,128)(2,1)}, bf16[256,1152]{1,0:T(8,128)(2,1)}, f32[3,3,1152]{2,1,0:T(4,128)}) custom-call(bf16[256,1152]{1,0:T(8,128)(2,1)S(1)} %get-tuple-element.14.gq, bf16[256,1152]{1,0:T(8,128)(2,1)S(1)} %get-tuple-element.15.gv, f32[256,1152]{1,0:T(8,128)S(1)} %get-tuple-element.16.dk, ...), custom_call_target="tpu_custom_call" | custom-call | tf_op jit(solution)/shard_map/pallas_call | solution.py:575

commit v4 on v3

--- a/solution.py
+++ b/solution.py
@@ -288,7 +288,9 @@
 
     loads[2].wait()
     for at in groups:
-        pq_turned[at, :] = jnp.maximum(qb[:, at], 0).T
+        pq = jnp.maximum(qb[:, at], 0)
+        pq_turned[at, :] = pq.T
+        weight[:, at] = pq.astype(F32)
 
     arrived(ks_plane, PLANE - 1, recv_sem.at[KS1])
     ks_line[z] = total(ks_plane[...]).astype(BF16)
@@ -348,8 +350,7 @@
     arrived(ks_line, line_size - 1, recv_sem.at[KS2])
     keysum = total(ks_line[...]) * (1.0 / count)
     for i, at in enumerate(groups):
-        pq = jnp.maximum(qb[:, at], 0).astype(F32)
-        weighted = split(pq * keysum[i : i + 1])
+        weighted = split(weight[:, at] * keysum[i : i + 1])
         den = jnp.dot(weighted, ones_twice, preferred_element_type=F32) + DEN_EPS
         inv = pl.reciprocal(den, approx=True)
         inv = inv * (2.0 - den * inv)
@@ -372,7 +373,7 @@
 
     for at in groups:
         inv = inv_den[:, at]
-        weight[:, at] = jnp.maximum(qb[:, at].astype(F32), 0.0) * (inv * inv)
+        weight[:, at] = weight[:, at] * (inv * inv)
 
     @pl.when(owned(TAP_OWNERS, GROUPS))
     def _():
@@ -497,7 +498,7 @@
     ]
     for store in stores:
         store.start()
-    parts = 3
+    parts = 1
     wide = CHANNELS // parts
     for p in range(parts):
         for i in range(p * (GROUPS // parts), (p + 1) * (GROUPS // parts)):
@@ -585,7 +586,7 @@
         scratch_shapes=[
             pltpu.VMEM(flat, BF16),
             pltpu.SemaphoreType.DMA((3,)),
-            pltpu.SemaphoreType.DMA((3,)),
+            pltpu.SemaphoreType.DMA((1,)),
         ],
         compiler_params=pltpu.CompilerParams(vmem_limit_bytes=32 * 1024 * 1024),
     )(gq, gv, dk, gw, kb, gks)

time: 49.8 us -> 49.8 us (level)
  no operation moved by 1% of the time
where the time goes in v4:
time: 49.8 us; the launch traced here: 49.7 us
  Pallas kernels  49 us (98%)
  between operations  0.64 us (1%)
    pallas_call x1, Pallas kernels, shards(): pl.pallas_call(functools.partial(exchange_kernel, sizes), out_shape=(jax....  47.8 us
    pallas_call x1, Pallas kernels, shards(): pl.pallas_call(finish_kernel, out_shape=(jax.ShapeDtypeStruct(flat, BF16)...  1.26 us

profile of v4, /device:TPU:1, one launch (start us, length us, event | category | flops | bytes accessed | tf_op | source)
XLA Modules:
  0.0 49.7 jit_solution(9717139257374034630)
XLA Ops:
  0.6 47.8 %shard_map.84 = (bf16[256,1152]{1,0:T(8,128)(2,1)S(1)}, bf16[256,1152]{1,0:T(8,128)(2,1)S(1)}, f32[256,1152]{1,0:T(8,128)S(1)}, f32[3,3,1152]{2,1,0:T(4,128)S(1)...) custom-call(bf16[256,1152]{1,0:T(8,128)(2,1)} %bitcast.7, bf16[256,1152]{1,0:T(8,128)(2,1)} %bitcast.8, ...), custom_call_target="tpu_custom_call" | custom-call | tf_op jit(solution)/shard_map/pallas_call | solution.py:534
  48.4 1.3 %shard_map.85 = (bf16[256,1152]{1,0:T(8,128)(2,1)}, bf16[256,1152]{1,0:T(8,128)(2,1)}, bf16[256,1152]{1,0:T(8,128)(2,1)}, f32[3,3,1152]{2,1,0:T(4,128)}) custom-call(bf16[256,1152]{1,0:T(8,128)(2,1)S(1)} %get-tuple-element.14.gq, bf16[256,1152]{1,0:T(8,128)(2,1)S(1)} %get-tuple-element.15.gv, f32[256,1152]{1,0:T(8,128)S(1)} %get-tuple-element.16.dk, ...), custom_call_target="tpu_custom_call" | custom-call | tf_op jit(solution)/shard_map/pallas_call | solution.py:576
